TPU v7x, 32 devices: a whole 2x2x4 slice. The times are simulated.
32 devices in a mesh: req: 4 (over y, x), mlp: 8 (over z, core).
Axes of the slice: x: 2, y: 2, z: 4, core: 2. Of those that a mesh axis runs over, the one named last changes fastest.
Arguments:
- hidden: bfloat16 [8, 5, 4096], P('req', None, 'mlp'), may hold values from -6 to 6
- attn_gain: float32 [4096], P('mlp'), may hold values from 0.1 to 1.9
- w_qkv: bfloat16 [4096, 6144], P('mlp'), may hold values from -0.09375 to 0.09375
- w_out: bfloat16 [4096, 4096], P(None, 'mlp'), may hold values from -0.09375 to 0.09375
- mlp_gain: float32 [4096], replicated, may hold values from 0.1 to 1.9
- w_gate: bfloat16 [4096, 14336], P(None, ('req', 'mlp')), may hold values from -0.09375 to 0.09375
- w_up: bfloat16 [4096, 14336], P(None, ('req', 'mlp')), may hold values from -0.09375 to 0.09375
- w_down: bfloat16 [14336, 4096], P(('req', 'mlp')), may hold values from -0.09375 to 0.09375
- kv_cache: bfloat16 [8, 1024, 2048], P('req', 'mlp')
- lengths: int32 [8], P('req'), may hold values from 1 to 1024, as said below
- mig_slot: int32 [4], replicated, may hold values from 0 to 1, as said below
- mig_dest: int32 [4], replicated, may hold values from 0 to 3, each once
Outputs:
- layer_out: bfloat16 [8, 5, 4096], P('req', None, 'mlp')
- moved_cache: bfloat16 [4, 128, 2048], P('req', 'mlp')
Inputs may be any that keep to these rules, and one draw needn't show every extreme that they name: `mig_slot`: the slot of each group that its leaving request vacates and the arriving one takes. `mig_dest`: A permutation of the groups: every group receives exactly one request. `lengths`: in slot g * 2 + mig_slot[g] the length is at most 128, reached in some group; some slot has exactly 1024.
All inputs are finite; a program needn't handle non-finite values.
Results may differ from a plain program's by a relative error of at most 0.012.
The roundings to bfloat16 on the way count: a program that leaves them out, or rounds other values in their place, can miss the bound.
Values may be sent and summed in bfloat16 or wider, within the bound.
A program may use at most 128 MiB of HBM per device.

v0:
```python
import jax
import jax.numpy as jnp
from jax import lax
from jax.sharding import PartitionSpec as P

D = 4096
HEADS = 32
KVH = 8
HD = 128
MIG_ROWS = 16
EPSILON = 1e-05
ROPE_BASE = 500000.0
NEG_FILL = -1e30


def merged_2(shard, axis, combine):
    everything = jax.tree.map(lambda part: lax.all_gather(part, axis), shard)
    initial = jax.tree.map(lambda part: part[0], everything)

    def lap(k, so_far):
        return combine(so_far, jax.tree.map(lambda part: part[k], everything))

    return lax.fori_loop(1, lax.axis_size(axis), lap, initial)


def rotate(vectors, positions):
    half_dim = vectors.shape[-1] // 2
    frequency = ROPE_BASE ** (-(jnp.arange(half_dim).astype(jnp.float32) / half_dim))
    angles = positions.astype(jnp.float32)[..., None, None] * frequency
    cos_part = jnp.cos(angles)
    sin_part = jnp.sin(angles)
    leading = vectors[..., :half_dim]
    trailing = vectors[..., half_dim:]
    return jnp.concatenate(
        [leading * cos_part - trailing * sin_part, trailing * cos_part + leading * sin_part],
        axis=-1,
    )


def combine(former, latter):
    former_max, former_sum, former_acc = former
    latter_max, latter_sum, latter_acc = latter
    highest = jnp.maximum(former_max, latter_max)
    former_rate = jnp.exp(former_max - highest)
    latter_rate = jnp.exp(latter_max - highest)
    return (
        highest,
        former_sum * former_rate + latter_sum * latter_rate,
        former_acc * former_rate[..., None] + latter_acc * latter_rate[..., None],
    )


def softmax_part(scores, usable, values, pattern):
    highest = jnp.max(jnp.where(usable, scores, NEG_FILL), axis=-1)
    weights = jnp.where(usable, jnp.exp(scores - highest[..., None]), 0.0)
    mixture = jnp.einsum(
        pattern, weights.astype(jnp.bfloat16), values, preferred_element_type=jnp.float32
    )
    return (highest, jnp.sum(weights, axis=-1), mixture)


def body(
    hidden,
    attn_gain,
    w_qkv,
    w_out,
    mlp_gain,
    w_gate,
    w_up,
    w_down,
    kv_cache,
    lengths,
    mig_slot,
    mig_dest,
):
    group_count = lax.axis_size("req")
    block_count = lax.axis_size("mlp")
    group_id = lax.axis_index("req")
    block_id = lax.axis_index("mlp")
    slot_count, spec_len, width_dev = hidden.shape
    ctx_dev = kv_cache.shape[1]
    kv_width = kv_cache.shape[2] // 2
    zero_index = jnp.zeros((), jnp.int32)
    own_slot = mig_slot[group_id]
    target = mig_dest[group_id]
    source = jnp.sum(jnp.where(mig_dest == group_id, jnp.arange(group_count, dtype=jnp.int32), 0))
    leaving = lax.dynamic_index_in_dim(kv_cache, own_slot, 0, keepdims=False)[:MIG_ROWS]
    outgoing = jnp.zeros((group_count,) + leaving.shape, leaving.dtype)
    outgoing = lax.dynamic_update_slice(outgoing, leaving[None], (target, zero_index, zero_index))
    incoming = lax.all_to_all(outgoing, "req", split_axis=0, concat_axis=0, tiled=True)
    arrived = lax.dynamic_index_in_dim(incoming, source, 0, keepdims=False)
    live_cache = lax.dynamic_update_slice(
        kv_cache, arrived[None], (own_slot, zero_index, zero_index)
    )
    widened = hidden.astype(jnp.float32)
    square_part = jnp.sum(widened * widened, axis=-1)
    scaled = (widened * attn_gain).astype(jnp.bfloat16)
    projected = jnp.einsum("rsd,de->rse", scaled, w_qkv, preferred_element_type=jnp.float32)
    square_sum, projected = lax.psum((square_part, projected), "mlp")
    projected = projected * lax.rsqrt(square_sum / D + EPSILON)[..., None]
    positions = lengths[:, None] + jnp.arange(spec_len, dtype=jnp.int32)[None, :]
    query_width = HEADS * HD
    queries = rotate(
        projected[..., :query_width].reshape(slot_count, spec_len, HEADS, HD), positions
    ).astype(jnp.bfloat16)
    new_keys = rotate(
        projected[..., query_width : query_width + kv_width].reshape(slot_count, spec_len, KVH, HD),
        positions,
    ).astype(jnp.bfloat16)
    new_values = (
        projected[..., query_width + kv_width :]
        .reshape(slot_count, spec_len, KVH, HD)
        .astype(jnp.bfloat16)
    )
    grouped = queries.reshape(slot_count, spec_len, KVH, HEADS // KVH, HD)
    score_scale = HD ** (-0.5)
    cached_keys = live_cache[..., :kv_width].reshape(slot_count, ctx_dev, KVH, HD)
    cached_values = live_cache[..., kv_width:].reshape(slot_count, ctx_dev, KVH, HD)
    scores = (
        jnp.einsum("rsgqd,rcgd->rgsqc", grouped, cached_keys, preferred_element_type=jnp.float32)
        * score_scale
    )
    stored = jnp.arange(ctx_dev, dtype=jnp.int32) * block_count + block_id
    usable = (stored[None, :] < lengths[:, None])[:, None, None, None, :]
    block_part = softmax_part(scores, usable, cached_values, "rgsqc,rcgd->rgsqd")
    merged = merged_2(block_part, "mlp", combine)
    own_scores = (
        jnp.einsum("rsgqd,rtgd->rgsqt", grouped, new_keys, preferred_element_type=jnp.float32)
        * score_scale
    )
    causal = (jnp.arange(spec_len)[:, None] >= jnp.arange(spec_len)[None, :])[
        None, None, :, None, :
    ]
    own_part = softmax_part(own_scores, causal, new_values, "rgsqt,rtgd->rgsqd")
    highest, summed, mixture = combine(merged, own_part)
    attended = (
        (mixture / summed[..., None])
        .transpose(0, 2, 1, 3, 4)
        .reshape(slot_count, spec_len, query_width)
        .astype(jnp.bfloat16)
    )
    residual = (
        widened + jnp.einsum("rse,ed->rsd", attended, w_out, preferred_element_type=jnp.float32)
    ).astype(jnp.bfloat16)
    gathered = lax.all_gather(residual[None], ("req", "mlp"), axis=0, tiled=True)
    token_group = slot_count * spec_len
    gathered = gathered.reshape(group_count, block_count, token_group, width_dev)
    widened_rows = gathered.astype(jnp.float32)
    inverse = lax.rsqrt(jnp.sum(widened_rows * widened_rows, axis=(1, 3)) / D + EPSILON)
    scaled_rows = (widened_rows * mlp_gain.reshape(block_count, 1, width_dev)).astype(jnp.bfloat16)
    hidden_dev = w_gate.shape[1]
    gate_proj = (
        jnp.einsum(
            "rmtc,mcf->rtf",
            scaled_rows,
            w_gate.reshape(block_count, width_dev, hidden_dev),
            preferred_element_type=jnp.float32,
        )
        * inverse[..., None]
    )
    up_proj = (
        jnp.einsum(
            "rmtc,mcf->rtf",
            scaled_rows,
            w_up.reshape(block_count, width_dev, hidden_dev),
            preferred_element_type=jnp.float32,
        )
        * inverse[..., None]
    )
    activated = (jax.nn.silu(gate_proj) * up_proj).astype(jnp.bfloat16)
    down_cols = w_down.reshape(hidden_dev, block_count, width_dev)
    block_index = jnp.arange(
        lax.axis_size(("req", "mlp")) * token_group // token_group, dtype=jnp.int32
    )
    row_sel = jnp.take(activated, block_index // block_count, axis=0)
    col_sel = jnp.take(down_cols, block_index % block_count, axis=1)
    product = jnp.einsum("ktf,fkc->ktc", row_sel, col_sel, preferred_element_type=jnp.float32)
    added = lax.psum_scatter(
        product.reshape(lax.axis_size(("req", "mlp")) * token_group, width_dev),
        ("req", "mlp"),
        scatter_dimension=0,
        tiled=True,
    )
    layer_out = (
        residual.astype(jnp.float32) + added.reshape(slot_count, spec_len, width_dev)
    ).astype(jnp.bfloat16)
    return (layer_out, arrived[None])


def solution(mesh):
    placed = (
        P("req", None, "mlp"),
        P("mlp"),
        P("mlp", None),
        P(None, "mlp"),
        P(),
        P(None, ("req", "mlp")),
        P(None, ("req", "mlp")),
        P(("req", "mlp"), None),
        P("req", "mlp", None),
        P("req"),
        P(),
        P(),
    )
    return jax.shard_map(
        body,
        mesh=mesh,
        in_specs=placed,
        out_specs=(P("req", None, "mlp"), P("req", "mlp", None)),
        check_vma=False,
    )
```

profile of v0, /device:TPU:0, one launch (start us, length us, event | category | flops | bytes accessed | tf_op | source)
XLA Modules:
  0.0 325.4 jit_solution(10649896896473231463)
XLA Ops:
  7.3 4.6 %fusion.9 = f32[2,5,6144]{2,1,0:T(8,128)} fusion(bf16[512,6144]{1,0:T(8,128)(2,1)} %param.16, bf16[2,5,512]{2,0,1:T(2,128)(2,1)} %param.14, f32[512]{0:T(512)} %param.15), kind=kOutput, calls=%fused_computation.17 | convolution fusion | flops 62929920 | bytes 6549504 | tf_op jit(solution)/shard_map/rsd,de->rse/dot_general | solution.py:98
  11.9 0.6 dynamic_slice.46
  13.8 0.6 dynamic_slice.44
  17.0 0.7 broadcast_in_dim.99
  17.7 0.6 dynamic-slice_dynamic-update-slice_fusion
  18.4 5.2 %all-to-all-start = ((bf16[4,16,2048]{2,1,0:T(8,128)(2,1)}), bf16[4,16,2048]{2,1,0:T(8,128)(2,1)S(1)}, u32[]{:S(2)}, u32[]{:S(2)}) async-start(bf16[4,16,2048]{2,1,0:T(8,128)(2,1)} %dynamic-slice_dynamic-update-slice_fusion), calls=%async_computation | async-start | bytes 524288 | tf_op jit(solution)/shard_map/all_to_all | solution.py:90
  23.6 0.7 copy.134
  24.3 0.6 fusion.56
  26.2 16.4 %psum.15 = f32[2,5]{1,0:T(2,128)S(1)} all-reduce(f32[2,5]{1,0:T(2,128)S(1)} %fusion.47), channel_id=1, replica_groups=mesh['req'=4,'mlp'=8] {'mlp'}, use_global_device_ids=true, to_apply=%region_2.3 | all-reduce | flops 10 | bytes 80 | tf_op jit(solution)/shard_map/psum | solution.py:99
  43.6 26.7 %all-reduce.4.cloned.1.call-done = f32[2,5,6144]{2,1,0:T(8,128)} async-done(((f32[2,5,6144]{2,1,0:T(8,128)}), f32[2,5,6144]{2,1,0:T(8,128)}) %all-reduce.4.cloned.1.call-update) | async-done | bytes 245776 | tf_op jit(solution)/shard_map/psum | solution.py:99
  70.3 1.1 broadcast_multiply_fusion
  71.9 0.3 copy.184
  72.1 2.0 dynamic_update_slice.7
  74.2 0.4 select_reduce_fusion
  74.6 0.4 fusion.37
  75.0 0.8 copy.139
  75.9 4.2 %copy.227 = bf16[56,8,8,512]{3,2,0,1:T(8,128)(2,1)} copy(bf16[56,8,8,512]{3,2,1,0:T(8,128)(2,1)} %bitcast.134) | data formatting | bytes 7340032 | tf_op jit(solution)/shard_map/reshape | solution.py:171
  80.1 9.3 %gather_fusion.1 = bf16[32,448,512]{2,1,0:T(8,128)(2,1)} fusion(bf16[448,8,512]{2,0,1:T(8,128)(2,1)} %bitcast.133, s32[1024]{0:T(1024)S(1)} %pad_clamp_fusion), kind=kCustom, calls=%fused_computation.1 | custom fusion | bytes 29360256 | tf_op jit(solution)/shard_map/jit(_take)/gather | solution.py:176
  89.6 0.7 fusion.48
  90.3 0.4 copy.145
  91.1 0.4 copy.152
  91.7 14.0 %all-gather = f32[16,8,5,4]{1,3,2,0:T(4,128)S(1)} all-gather(f32[2,8,5,4]{1,3,2,0:T(4,128)S(1)} %copy.136), channel_id=2, replica_groups=mesh['req'=4,'mlp'=8] {'mlp'}, dimensions={0}, use_global_device_ids=true | all-gather | bytes 11520 | tf_op jit(solution)/shard_map/all_gather | solution.py:17
  105.7 0.3 fusion.36
  106.2 14.0 %all-gather.1 = f32[16,8,5,4]{1,3,2,0:T(4,128)S(1)} all-gather(f32[2,8,5,4]{1,3,2,0:T(4,128)S(1)} %copy.137), channel_id=3, replica_groups=mesh['req'=4,'mlp'=8] {'mlp'}, dimensions={0}, use_global_device_ids=true | all-gather | bytes 11520 | tf_op jit(solution)/shard_map/all_gather | solution.py:17
  120.2 0.9 slice.68
  121.2 12.6 %while.19 = (s32[]{:T(128)}, f32[2,8,5,4]{1,3,2,0:T(4,128)S(1)}, f32[2,8,5,4]{1,3,2,0:T(4,128)S(1)}, f32[2,8,5,4,128]{4,3,2,1,0:T(4,128)S(1)}, f32[8,2,8,5,4]{2,...) while((s32[]{:T(128)}, f32[2,8,5,4]{1,3,2,0:T(4,128)S(1)}, ...), condition=%wide.region_7.8_spmd, body=%wide.region_6.7_spmd.sunk | while | flops 124805 | bytes 837271 | solution.py:23
  121.2 0.9 constant_dynamic-slice_fusion.4
  122.2 0.1 copy.232
  122.3 0.1 copy.233
  122.4 0.5 fusion.73
  123.0 0.9 constant_dynamic-slice_fusion.4
  124.0 0.1 copy.232
  124.1 0.1 copy.233
  124.2 0.5 fusion.73
  124.8 0.9 constant_dynamic-slice_fusion.4
  125.8 0.1 copy.232
  125.9 0.1 copy.233
  126.0 0.5 fusion.73
  126.6 0.9 constant_dynamic-slice_fusion.4
  127.6 0.1 copy.232
  127.7 0.1 copy.233
  127.8 0.5 fusion.73
  128.4 0.9 constant_dynamic-slice_fusion.4
  129.4 0.1 copy.232
  129.5 0.1 copy.233
  129.6 0.5 fusion.73
  130.2 0.9 constant_dynamic-slice_fusion.4
  131.2 0.1 copy.232
  131.4 0.5 fusion.73
  132.0 0.9 constant_dynamic-slice_fusion.4
  133.0 0.1 copy.232
  133.2 0.5 fusion.73
  134.1 0.3 fusion.19
  134.4 2.9 fusion.29
  137.3 41.9 %all-gather.3 = bf16[64,5,512]{2,1,0:T(8,128)(2,1)S(1)} all-gather(bf16[2,5,512]{2,1,0:T(8,128)(2,1)S(1)} %fusion.29), channel_id=5, replica_groups=mesh['req'=4,'mlp'=8] {'req','mlp'}, dimensions={0}, use_global_device_ids=true | all-gather | bytes 337920 | tf_op jit(solution)/shard_map/all_gather | solution.py:145
  179.3 0.2 multiply_reduce_fusion
  179.6 3.4 %fusion.24 = f32[4,10,448]{2,1,0:T(8,128)S(1)} fusion(bf16[56,8,8,512]{3,2,1,0:T(8,128)(2,1)} %bitcast.153, f32[4,8,10,512]{3,2,1,0:T(8,128)S(1)} %reshape.225, f32[8,512]{1,0:T(8,128)S(1)} %mul.286, f32[4,10]{1,0:T(4,128)S(1)} %add_rsqrt_fusion), kind=kOutput, calls=%fused_computation.37 | convolution fusion | flops 147146240 | bytes 4413600 | tf_op jit(solution)/shard_map/rmtc,mcf->rtf/dot_general | solution.py:153
  183.0 1.2 fusion.25
  184.2 0.6 gather_fusion
  184.8 6.5 %fusion.4 = f32[32,10,512]{2,1,0:T(8,128)S(1)} fusion(bf16[32,448,512]{2,1,0:T(8,128)(2,1)} %gather_fusion.1, pred[32]{0:T(512)(128)(4,1)S(1)} %get-tuple-element.263, bf16[32,10,448]{2,1,0:T(8,128)(2,1)S(1)} %gather_fusion, pred[32]{0:T(512)(128)(4,1)S(1)} %get-tuple-element.264), kind=kOutput, calls=%fused_computation.12 | convolution fusion | flops 154284032 | bytes 15622208 | tf_op jit(solution)/shard_map/ktf,fkc->ktc/dot_general | solution.py:177
  191.2 0.9 reshape.223
  192.2 125.3 %all-reduce.6.cloned.1.call-done = f32[320,512]{1,0:T(8,128)} async-done(((f32[320,512]{1,0:T(8,128)}), f32[320,512]{1,0:T(8,128)}) %all-reduce.6.cloned.1.call-update) | async-done | bytes 655376
  317.5 0.8 constant_dynamic-slice_fusion.2
  318.3 0.6 copy.159
  (79 shorter events, 3.1 us)
Async XLA Ops:
  7.2 16.4 %copy-start.2 = (bf16[2,5,512]{2,0,1:T(2,128)(2,1)S(1)}, bf16[2,5,512]{2,0,1:T(2,128)(2,1)}, u32[]{:S(2)}) copy-start(bf16[2,5,512]{2,0,1:T(2,128)(2,1)} %param.14) | copy-start | bytes 30724
  7.2 4.7 %copy-start.6 = (s32[4]{0:T(128)S(1)}, s32[4]{0:T(128)}, u32[]{:S(2)}) copy-start(s32[4]{0:T(128)} %param.25) | copy-start | bytes 52
  7.2 6.6 %copy-start.5 = (s32[4]{0:T(128)S(1)}, s32[4]{0:T(128)}, u32[]{:S(2)}) copy-start(s32[4]{0:T(128)} %param.24) | copy-start | bytes 52
  7.2 10.5 %copy-start = (bf16[2,128,2048]{2,1,0:T(8,128)(2,1)S(1)}, bf16[2,128,2048]{2,1,0:T(8,128)(2,1)}, u32[]{:S(2)}) copy-start(bf16[2,128,2048]{2,1,0:T(8,128)(2,1)} %param.22) | copy-start | bytes 3145732
  7.2 35.4 %copy-start.7 = (s32[2]{0:T(128)S(1)}, s32[2]{0:T(128)}, u32[]{:S(2)}) copy-start(s32[2]{0:T(128)} %param.23) | copy-start | bytes 28
  7.2 63.1 %all-reduce.4.cloned.1.call-start = ((), (), s32[]{:S(2)}) async-start(), calls=%async_computation.1 | async-start | bytes 786432 | tf_op jit(solution)/shard_map/psum | solution.py:99
  18.4 53.5 %all-to-all-start = ((bf16[4,16,2048]{2,1,0:T(8,128)(2,1)}), bf16[4,16,2048]{2,1,0:T(8,128)(2,1)S(1)}, u32[]{:S(2)}, u32[]{:S(2)}) async-start(bf16[4,16,2048]{2,1,0:T(8,128)(2,1)} %dynamic-slice_dynamic-update-slice_fusion), calls=%async_computation | async-start | bytes 524288 | tf_op jit(solution)/shard_map/all_to_all | solution.py:90
  23.5 96.7 %all-gather.6.cloned.1.call-start = ((), (), s32[]{:S(2)}) async-start(), calls=%async_computation.2 | async-start | bytes 1474560 | tf_op jit(solution)/shard_map/all_gather | solution.py:17
  71.9 8.2 %copy-start.1 = (bf16[1,16,2048]{2,1,0:T(8,128)(2,1)}, bf16[1,16,2048]{2,1,0:T(8,128)(2,1)S(1)}, u32[]{:S(2)}) copy-start(bf16[1,16,2048]{2,1,0:T(8,128)(2,1)S(1)} %constant_dynamic-slice_fusion.1) | copy-start | bytes 196612
  75.0 5.0 %copy-start.3 = (f32[4096]{0:T(1024)S(1)}, f32[4096]{0:T(1024)}, u32[]{:S(2)}) copy-start(f32[4096]{0:T(1024)} %param.18) | copy-start | bytes 49156
  75.9 241.6 %all-reduce.6.cloned.1.call-start = ((), (), s32[]{:S(2)}) async-start(), calls=%async_computation.3 | async-start | bytes 1310720
  179.6 3.4 %copy-start.4 = (bf16[4096,448]{0,1:T(8,128)(2,1)S(1)}, bf16[4096,448]{0,1:T(8,128)(2,1)}, u32[]{:S(2)}) copy-start(bf16[4096,448]{0,1:T(8,128)(2,1)} %param.20) | copy-start | bytes 11010052
Sparse Core Ops, SparseCore 0:
  12.0 58.2 all-reduce.3
  76.0 23.0 all-gather.5
  192.3 125.1 all-reduce.5
where the time goes:
time: 326 us; the launch traced here: 325 us
  waiting for transfers between devices  152 us (47%)
  blocking collectives  86.3 us (26%)
  local copies, waits for them, and re-layouts  34.3 us (11%)
  matrix products  20.4 us (6%)
  between operations  19.9 us (6%)
  other arithmetic  7.03 us (2%)
  starting transfers between devices  5.26 us (2%)
    unnamed x4, waiting for transfers between devices  125 us
    all_gather x1, blocking collectives, body(): lax.all_gather(residual[None], ('req', 'mlp'), axis=0, tiled=True)  41.9 us
    all_gather x2, blocking collectives, merged_2(): everything = jax.tree.map(lambda part: lax.all_gather(part, axis), shard)  28 us
    psum x1, waiting for transfers between devices, body(): square_sum, projected = lax.psum((square_part, projected), 'mlp')  26.7 us
    psum x1, blocking collectives, body(): square_sum, projected = lax.psum((square_part, projected), 'mlp')  16.4 us
    gather x1, local copies, waits for them, and re-layouts, body(): col_sel = jnp.take(down_cols, block_index % block_count, axis=1)  9.3 us
    dynamic_slice x7, local copies, waits for them, and re-layouts, lap(): return combine(so_far, jax.tree.map(lambda part: part[k], everything))  6.53 us
  transfers between devices with their start and end apart: 4, of which 2 were waited for; matrix products, arithmetic and copies ran while one was open for 7% of the time, Pallas kernels for 0%

commit v1 on v0

--- a/solution.py
+++ b/solution.py
@@ -11,6 +11,18 @@
 EPSILON = 1e-05
 ROPE_BASE = 500000.0
 NEG_FILL = -1e30
+
+
+def doubled_up(array, axis, dim):
+    ways, here, step = (lax.axis_size(axis), lax.axis_index(axis), array.shape[dim])
+    line, have = (array, 1)
+    while have < ways:
+        line = jnp.concatenate(
+            [line, lax.ppermute(line, axis, [(d, (d - have) % ways) for d in range(ways)])],
+            axis=dim,
+        )
+        have = 2 * have
+    return jnp.roll(line, here * step, axis=dim)
 
 
 def merged_2(shard, axis, combine):
@@ -142,7 +154,7 @@
     residual = (
         widened + jnp.einsum("rse,ed->rsd", attended, w_out, preferred_element_type=jnp.float32)
     ).astype(jnp.bfloat16)
-    gathered = lax.all_gather(residual[None], ("req", "mlp"), axis=0, tiled=True)
+    gathered = doubled_up(residual[None], ("req", "mlp"), 0)
     token_group = slot_count * spec_len
     gathered = gathered.reshape(group_count, block_count, token_group, width_dev)
     widened_rows = gathered.astype(jnp.float32)

time: 326 us -> 313 us (0.960)
  blocking collectives: 86.3 us -> 45 us
  waiting for transfers between devices: 152 us -> 173 us
  starting transfers between devices: 5.26 us -> 11.1 us
    all_gather x1 -> x0, blocking collectives: 41.9 us -> none  [body(): lax.all_gather(residual[None], ('req', 'mlp'), axis=0, tiled=True)]
    ppermute x0 -> x5, waiting for transfers between devices: none -> 14.6 us  [doubled_up(): lax.ppermute(line, axis, [(d, (d - have) % ways) for d in range(ways)])]
    unnamed x4, waiting for transfers between devices: 125 us -> 132 us
    ppermute x0 -> x5, starting transfers between devices: none -> 5.89 us  [doubled_up(): lax.ppermute(line, axis, [(d, (d - have) % ways) for d in range(ways)])]
  transfers between devices with their start and end apart: 4 -> 9, of which waited for: 2 -> 6; matrix products, arithmetic and copies ran while one was open for 7% -> 7% of each run, Pallas kernels for 0% -> 0%
where the time goes in v1:
time: 313 us; the launch traced here: 312 us
  waiting for transfers between devices  173 us (55%)
  blocking collectives  45 us (14%)
  local copies, waits for them, and re-layouts  34.7 us (11%)
  matrix products  20.4 us (7%)
  between operations  20 us (6%)
  starting transfers between devices  11.1 us (4%)
  other arithmetic  7.39 us (2%)
    unnamed x4, waiting for transfers between devices  132 us
    all_gather x2, blocking collectives, merged_2(): everything = jax.tree.map(lambda part: lax.all_gather(part, axis), shard)  28.6 us
    psum x1, waiting for transfers between devices, body(): square_sum, projected = lax.psum((square_part, projected), 'mlp')  26.7 us
    psum x1, blocking collectives, body(): square_sum, projected = lax.psum((square_part, projected), 'mlp')  16.4 us
    ppermute x5, waiting for transfers between devices, doubled_up(): lax.ppermute(line, axis, [(d, (d - have) % ways) for d in range(ways)])  14.6 us
    gather x1, local copies, waits for them, and re-layouts, body(): col_sel = jnp.take(down_cols, block_index % block_count, axis=1)  9.14 us
    dynamic_slice x7, local copies, waits for them, and re-layouts, lap(): return combine(so_far, jax.tree.map(lambda part: part[k], everything))  6.53 us
    dot_general x1, matrix products, body(): jnp.einsum('ktf,fkc->ktc', row_sel, col_sel, preferred_element_type=jnp.f...  6.45 us
  transfers between devices with their start and end apart: 9, of which 6 were waited for; matrix products, arithmetic and copies ran while one was open for 7% of the time, Pallas kernels for 0%

profile of v1, /device:TPU:0, one launch (start us, length us, event | category | flops | bytes accessed | tf_op | source)
XLA Modules:
  0.0 311.8 jit_solution(6770497114858041925)
XLA Ops:
  7.3 4.6 %fusion.9 = f32[2,5,6144]{2,1,0:T(8,128)} fusion(bf16[512,6144]{1,0:T(8,128)(2,1)} %param.16, bf16[2,5,512]{2,0,1:T(2,128)(2,1)} %param.14, f32[512]{0:T(512)} %param.15), kind=kOutput, calls=%fused_computation.17 | convolution fusion | flops 62929920 | bytes 6549504 | tf_op jit(solution)/shard_map/rsd,de->rse/dot_general | solution.py:110
  11.9 0.6 dynamic_slice.50
  13.8 0.6 dynamic_slice.48
  17.0 0.7 broadcast_in_dim.99
  17.7 0.6 dynamic-slice_dynamic-update-slice_fusion
  18.4 5.2 %all-to-all-start = ((bf16[4,16,2048]{2,1,0:T(8,128)(2,1)}), bf16[4,16,2048]{2,1,0:T(8,128)(2,1)S(1)}, u32[]{:S(2)}, u32[]{:S(2)}) async-start(bf16[4,16,2048]{2,1,0:T(8,128)(2,1)} %dynamic-slice_dynamic-update-slice_fusion), calls=%async_computation | async-start | bytes 524288 | tf_op jit(solution)/shard_map/all_to_all | solution.py:102
  23.6 0.7 copy.144
  24.3 0.6 fusion.58
  26.2 16.4 %psum.15 = f32[2,5]{1,0:T(2,128)S(1)} all-reduce(f32[2,5]{1,0:T(2,128)S(1)} %fusion.49), channel_id=1, replica_groups=mesh['req'=4,'mlp'=8] {'mlp'}, use_global_device_ids=true, to_apply=%region_2.3 | all-reduce | flops 10 | bytes 80 | tf_op jit(solution)/shard_map/psum | solution.py:111
  43.6 26.7 %all-reduce.4.cloned.1.call-done = f32[2,5,6144]{2,1,0:T(8,128)} async-done(((f32[2,5,6144]{2,1,0:T(8,128)}), f32[2,5,6144]{2,1,0:T(8,128)}) %all-reduce.4.cloned.1.call-update) | async-done | bytes 245776 | tf_op jit(solution)/shard_map/psum | solution.py:111
  70.3 1.1 broadcast_multiply_fusion
  71.9 0.3 copy.203
  72.2 2.0 dynamic_update_slice.7
  74.2 0.4 select_reduce_fusion
  74.7 0.4 fusion.39
  75.1 0.8 copy.149
  76.1 0.7 fusion.50
  76.8 0.4 copy.155
  77.6 0.4 copy.162
  78.2 14.6 %all-gather = f32[16,8,5,4]{1,3,2,0:T(4,128)S(1)} all-gather(f32[2,8,5,4]{1,3,2,0:T(4,128)S(1)} %copy.146), channel_id=2, replica_groups=mesh['req'=4,'mlp'=8] {'mlp'}, dimensions={0}, use_global_device_ids=true | all-gather | bytes 11520 | tf_op jit(solution)/shard_map/all_gather | solution.py:29
  92.8 0.3 fusion.38
  93.2 14.0 %all-gather.1 = f32[16,8,5,4]{1,3,2,0:T(4,128)S(1)} all-gather(f32[2,8,5,4]{1,3,2,0:T(4,128)S(1)} %copy.147), channel_id=3, replica_groups=mesh['req'=4,'mlp'=8] {'mlp'}, dimensions={0}, use_global_device_ids=true | all-gather | bytes 11520 | tf_op jit(solution)/shard_map/all_gather | solution.py:29
  107.3 0.9 slice.68
  108.3 12.6 %while.19 = (s32[]{:T(128)}, f32[2,8,5,4]{1,3,2,0:T(4,128)S(1)}, f32[2,8,5,4]{1,3,2,0:T(4,128)S(1)}, f32[2,8,5,4,128]{4,3,2,1,0:T(4,128)S(1)}, f32[8,2,8,5,4]{2,...) while((s32[]{:T(128)}, f32[2,8,5,4]{1,3,2,0:T(4,128)S(1)}, ...), condition=%wide.region_7.8_spmd, body=%wide.region_6.7_spmd.sunk | while | flops 124805 | bytes 837271 | solution.py:35
  108.3 0.9 constant_dynamic-slice_fusion.4
  109.3 0.1 copy.260
  109.5 0.5 fusion.75
  110.1 0.9 constant_dynamic-slice_fusion.4
  111.1 0.1 copy.260
  111.3 0.5 fusion.75
  111.9 0.9 constant_dynamic-slice_fusion.4
  112.9 0.1 copy.260
  113.1 0.5 fusion.75
  113.7 0.9 constant_dynamic-slice_fusion.4
  114.7 0.1 copy.260
  114.9 0.5 fusion.75
  115.5 0.9 constant_dynamic-slice_fusion.4
  116.7 0.5 fusion.75
  117.3 0.9 constant_dynamic-slice_fusion.4
  118.5 0.5 fusion.75
  119.1 0.9 constant_dynamic-slice_fusion.4
  120.3 0.5 fusion.75
  121.1 0.3 fusion.19
  121.5 2.9 constant_dynamic-update-slice_fusion.4
  124.4 3.1 collective-permute-start
  127.5 1.4 collective-permute-done
  128.9 0.8 collective-permute-start.1
  129.7 3.2 %collective-permute-done.1 = bf16[2,2,5,512]{3,2,1,0:T(8,128)(2,1)S(1)} collective-permute-done((bf16[2,2,5,512]{3,2,1,0:T(8,128)(2,1)S(1)}, bf16[2,2,5,512]{3,2,1,0:T(8,128)(2,1)S(1)}, u32[]{:S(2)}, u32[]{:S(2)}) %collective-permute-start.1) | collective-permute-done | bytes 20512 | tf_op jit(solution)/shard_map/ppermute | solution.py:21
  133.0 5.1 %collective-permute-done.2 = bf16[4,2,5,512]{3,2,1,0:T(8,128)(2,1)S(1)} collective-permute-done((bf16[4,2,5,512]{3,2,1,0:T(8,128)(2,1)S(1)}, bf16[4,2,5,512]{3,2,1,0:T(8,128)(2,1)S(1)}, u32[]{:S(2)}, u32[]{:S(2)}) %collective-permute-start.2) | collective-permute-done | bytes 40992 | tf_op jit(solution)/shard_map/ppermute | solution.py:21
  138.2 1.3 collective-permute-start.3
  139.5 4.9 %collective-permute-done.3 = bf16[8,2,5,512]{3,2,1,0:T(8,128)(2,1)S(1)} collective-permute-done((bf16[8,2,5,512]{3,2,1,0:T(8,128)(2,1)S(1)}, bf16[8,2,5,512]{3,2,1,0:T(8,128)(2,1)S(1)}, u32[]{:S(2)}, u32[]{:S(2)}) %collective-permute-start.3) | collective-permute-done | bytes 81952 | tf_op jit(solution)/shard_map/ppermute | solution.py:21
  144.4 0.6 collective-permute-start.4
  145.0 4.2 %copy.255 = bf16[56,8,8,512]{3,2,0,1:T(8,128)(2,1)} copy(bf16[56,8,8,512]{3,2,1,0:T(8,128)(2,1)} %bitcast.152) | data formatting | bytes 7340032 | tf_op jit(solution)/shard_map/reshape | solution.py:183
  149.2 9.1 %gather_fusion.1 = bf16[32,448,512]{2,1,0:T(8,128)(2,1)} fusion(bf16[448,8,512]{2,0,1:T(8,128)(2,1)} %bitcast.151, s32[1024]{0:T(1024)S(1)} %pad_clamp_fusion), kind=kCustom, calls=%fused_computation.1 | custom fusion | bytes 29360256 | tf_op jit(solution)/shard_map/jit(_take)/gather | solution.py:188
  158.6 0.2 multiply_reduce_fusion
  158.9 0.4 copy.166
  159.7 3.4 %fusion.24 = f32[4,10,448]{2,1,0:T(8,128)S(1)} fusion(bf16[56,8,8,512]{3,2,1,0:T(8,128)(2,1)} %bitcast.176, bf16[4,8,10,512]{3,1,0,2:T(8,128)(2,1)S(1)} %multiply_convert_fusion, f32[4,10]{1,0:T(4,128)S(1)} %add_rsqrt_fusion), kind=kOutput, calls=%fused_computation.37 | convolution fusion | flops 146818560 | bytes 4069536 | tf_op jit(solution)/shard_map/rmtc,mcf->rtf/dot_general | solution.py:165
  163.1 1.2 fusion.25
  164.3 0.6 gather_fusion
  164.9 6.4 %fusion.4 = f32[32,10,512]{2,1,0:T(8,128)S(1)} fusion(bf16[32,448,512]{2,1,0:T(8,128)(2,1)} %gather_fusion.1, pred[32]{0:T(512)(128)(4,1)S(1)} %get-tuple-element.274, bf16[32,10,448]{2,1,0:T(8,128)(2,1)S(1)} %gather_fusion, pred[32]{0:T(512)(128)(4,1)S(1)} %get-tuple-element.275), kind=kOutput, calls=%fused_computation.12 | convolution fusion | flops 154284032 | bytes 15622208 | tf_op jit(solution)/shard_map/ktf,fkc->ktc/dot_general | solution.py:189
  171.3 0.9 reshape.223
  172.3 131.5 %all-reduce.6.cloned.1.call-done = f32[320,512]{1,0:T(8,128)} async-done(((f32[320,512]{1,0:T(8,128)}), f32[320,512]{1,0:T(8,128)}) %all-reduce.6.cloned.1.call-update) | async-done | bytes 655376
  303.9 0.8 constant_dynamic-slice_fusion.2
  304.7 0.6 copy.174
  (105 shorter events, 4.8 us)
Async XLA Ops:
  7.2 16.4 %copy-start.2 = (bf16[2,5,512]{2,0,1:T(2,128)(2,1)S(1)}, bf16[2,5,512]{2,0,1:T(2,128)(2,1)}, u32[]{:S(2)}) copy-start(bf16[2,5,512]{2,0,1:T(2,128)(2,1)} %param.14) | copy-start | bytes 30724
  7.2 4.7 %copy-start.6 = (s32[4]{0:T(128)S(1)}, s32[4]{0:T(128)}, u32[]{:S(2)}) copy-start(s32[4]{0:T(128)} %param.25) | copy-start | bytes 52
  7.2 6.6 %copy-start.5 = (s32[4]{0:T(128)S(1)}, s32[4]{0:T(128)}, u32[]{:S(2)}) copy-start(s32[4]{0:T(128)} %param.24) | copy-start | bytes 52
  7.2 10.5 %copy-start = (bf16[2,128,2048]{2,1,0:T(8,128)(2,1)S(1)}, bf16[2,128,2048]{2,1,0:T(8,128)(2,1)}, u32[]{:S(2)}) copy-start(bf16[2,128,2048]{2,1,0:T(8,128)(2,1)} %param.22) | copy-start | bytes 3145732
  7.2 35.4 %copy-start.7 = (s32[2]{0:T(128)S(1)}, s32[2]{0:T(128)}, u32[]{:S(2)}) copy-start(s32[2]{0:T(128)} %param.23) | copy-start | bytes 28
  7.2 63.1 %all-reduce.4.cloned.1.call-start = ((), (), s32[]{:S(2)}) async-start(), calls=%async_computation.1 | async-start | bytes 786432 | tf_op jit(solution)/shard_map/psum | solution.py:111
  18.4 53.5 %all-to-all-start = ((bf16[4,16,2048]{2,1,0:T(8,128)(2,1)}), bf16[4,16,2048]{2,1,0:T(8,128)(2,1)S(1)}, u32[]{:S(2)}, u32[]{:S(2)}) async-start(bf16[4,16,2048]{2,1,0:T(8,128)(2,1)} %dynamic-slice_dynamic-update-slice_fusion), calls=%async_computation | async-start | bytes 524288 | tf_op jit(solution)/shard_map/all_to_all | solution.py:102
  23.5 83.8 %all-gather.5.cloned.1.call-start = ((), (), s32[]{:S(2)}) async-start(), calls=%async_computation.2 | async-start | bytes 1474560 | tf_op jit(solution)/shard_map/all_gather | solution.py:29
  71.9 6.0 %copy-start.1 = (bf16[1,16,2048]{2,1,0:T(8,128)(2,1)}, bf16[1,16,2048]{2,1,0:T(8,128)(2,1)S(1)}, u32[]{:S(2)}) copy-start(bf16[1,16,2048]{2,1,0:T(8,128)(2,1)S(1)} %constant_dynamic-slice_fusion.1) | copy-start | bytes 196612
  75.9 228.0 %all-reduce.6.cloned.1.call-start = ((), (), s32[]{:S(2)}) async-start(), calls=%async_computation.3 | async-start | bytes 1310720
  124.4 4.6 %collective-permute-start = (bf16[1,2,5,512]{3,2,1,0:T(8,128)(2,1)S(1)}, bf16[1,2,5,512]{3,2,1,0:T(8,128)(2,1)S(1)}, u32[]{:S(2)}, u32[]{:S(2)}) collective-permute-start(bf16[1,2,5,512]{3,2,1,0:T(8,128)(2,1)S(1)} %bitcast.160), channel_id=1, source_target_pairs={{0,31},{1,0},{2,1},{3,2},{4,3},{5,4},{6,5},{7,6},{8,7},{9,8},{10,9... | collective-permute-start | bytes 30728 | tf_op jit(solution)/shard_map/ppermute | solution.py:21
  128.9 4.0 %collective-permute-start.1 = (bf16[2,2,5,512]{3,2,1,0:T(8,128)(2,1)S(1)}, bf16[2,2,5,512]{3,2,1,0:T(8,128)(2,1)S(1)}, u32[]{:S(2)}, u32[]{:S(2)}) collective-permute-start(bf16[2,2,5,512]{3,2,1,0:T(8,128)(2,1)S(1)} %pad_maximum_fusion.3), channel_id=1, source_target_pairs={{0,30},{1,31},{2,0},{3,1},{4,2},{5,3},{6,4},{7,5},{8,6},{9,7},{10,... | collective-permute-start | bytes 61448 | tf_op jit(solution)/shard_map/ppermute | solution.py:21
  132.9 16.3 %copy-start.3 = (f32[4096]{0:T(1024)S(1)}, f32[4096]{0:T(1024)}, u32[]{:S(2)}) copy-start(f32[4096]{0:T(1024)} %param.18) | copy-start | bytes 49156
  132.9 5.2 %collective-permute-start.2 = (bf16[4,2,5,512]{3,2,1,0:T(8,128)(2,1)S(1)}, bf16[4,2,5,512]{3,2,1,0:T(8,128)(2,1)S(1)}, u32[]{:S(2)}, u32[]{:S(2)}) collective-permute-start(bf16[4,2,5,512]{3,2,1,0:T(8,128)(2,1)S(1)} %pad_maximum_fusion.2), channel_id=1, source_target_pairs={{0,28},{1,29},{2,30},{3,31},{4,0},{5,1},{6,2},{7,3},{8,4},{9,5},{1... | collective-permute-start | bytes 122888 | tf_op jit(solution)/shard_map/ppermute | solution.py:21
  138.2 6.2 %collective-permute-start.3 = (bf16[8,2,5,512]{3,2,1,0:T(8,128)(2,1)S(1)}, bf16[8,2,5,512]{3,2,1,0:T(8,128)(2,1)S(1)}, u32[]{:S(2)}, u32[]{:S(2)}) collective-permute-start(bf16[8,2,5,512]{3,2,1,0:T(8,128)(2,1)S(1)} %pad_maximum_fusion.1), channel_id=1, source_target_pairs={{0,24},{1,25},{2,26},{3,27},{4,28},{5,29},{6,30},{7,31},{8,0},{9,1... | collective-permute-start | bytes 245768 | tf_op jit(solution)/shard_map/ppermute | solution.py:21
  144.4 14.0 %collective-permute-start.4 = (bf16[16,2,5,512]{3,2,1,0:T(8,128)(2,1)S(1)}, bf16[16,2,5,512]{3,2,1,0:T(8,128)(2,1)S(1)}, u32[]{:S(2)}, u32[]{:S(2)}) collective-permute-start(bf16[16,2,5,512]{3,2,1,0:T(8,128)(2,1)S(1)} %get-tuple-element.255), channel_id=1, source_target_pairs={{0,16},{1,17},{2,18},{3,19},{4,20},{5,21},{6,22},{7,23},{8,24},{9,... | collective-permute-start | bytes 491528 | tf_op jit(solution)/shard_map/ppermute | solution.py:21
  159.6 3.5 %copy-start.4 = (bf16[4096,448]{0,1:T(8,128)(2,1)S(1)}, bf16[4096,448]{0,1:T(8,128)(2,1)}, u32[]{:S(2)}) copy-start(bf16[4096,448]{0,1:T(8,128)(2,1)} %param.20) | copy-start | bytes 11010052
Sparse Core Ops, SparseCore 0:
  12.0 58.2 all-reduce.3
  76.0 23.4 all-gather.4
  172.4 131.3 all-reduce.5
